TPU v7x, 256 devices: a whole 4x4x8 slice. The times are simulated.
256 devices in a mesh: dp: 4 (over z_lo), space: 8 (over x, z_hi), tensor: 8 (over y, core).
Axes of the slice: x: 4, y: 4, z: 8 (z_hi: 2, z_lo: 4; z = z_hi * 4 + z_lo), core: 2. Of those that a mesh axis runs over, the one named last changes fastest.
Arguments:
- features: bfloat16 [4, 128, 64, 1024], P('dp', ('space', 'tensor')), may hold values from -6 to 6
- kernel: bfloat16 [3, 3, 1024, 1024], P(None, None, 'tensor'), may hold values from -0.0625 to 0.0625
- embedding: float32 [1000, 1024], P(None, 'tensor'), may hold values from -6 to 6
- labels: int32 [4], P('dp'), may hold values from 0 to 999
Outputs:
- weight_grad: float32 [3, 3, 1024, 1024], P(None, None, 'tensor')
- embed_grad: float32 [1000, 1024], P(None, 'tensor')
All inputs are finite; a program needn't handle non-finite values.
Results may differ from a plain program's by a relative error of at most 0.00033.
Values may be sent and summed in bfloat16 or wider, within the bound.
No kernel may reach another device: no remote copies, remote signals or barrier semaphores. Data moves between devices by JAX's collectives and lax.ppermute only.
A program may use at most 64 MiB of HBM per device.

v0:
```python
import math
import jax
import jax.numpy as jnp
from jax import lax
from jax.sharding import PartitionSpec as P

r1_factor = 1000.0


def padded_2(block, sides, width):
    for axis, dim in sides:
        count = lax.axis_size(axis)
        forward = [(i, i + 1) for i in range(count - 1)]
        backward = [(target, source) for source, target in forward]
        low = lax.ppermute(
            lax.slice_in_dim(block, block.shape[dim] - width, None, axis=dim), axis, forward
        )
        high = lax.ppermute(lax.slice_in_dim(block, 0, width, axis=dim), axis, backward)
        block = jnp.concatenate([low, block, high], axis=dim)
    return block


def conv_valid(padded, kern):
    return lax.conv_general_dilated(
        padded,
        kern,
        (1, 1),
        "VALID",
        dimension_numbers=("NHWC", "HWIO", "NHWC"),
        preferred_element_type=jnp.float32,
    )


def pad_cols(field):
    return jnp.pad(field, ((0, 0), (0, 0), (1, 1), (0, 0)))


def taps_of(padded, grad):
    row_count = grad.shape[1]
    col_count = grad.shape[2]
    flat_grad = grad.reshape(-1, grad.shape[3])
    outer = []
    for tap_row in range(3):
        inner = []
        for tap_col in range(3):
            window = padded[
                :, tap_row : tap_row + row_count, tap_col : tap_col + col_count, :
            ].reshape(-1, padded.shape[3])
            inner.append(
                lax.dot_general(
                    window, flat_grad, (((0,), (0,)), ((), ())), preferred_element_type=jnp.float32
                )
            )
        outer.append(jnp.stack(inner))
    return jnp.stack(outer)


def forward_conv(padded, kernel_cols):
    whole = lax.all_gather(padded, "tensor", axis=3, tiled=True)
    return conv_valid(whole, kernel_cols)


def body(features, kernel, embedding, labels):
    tensor_count = lax.axis_size("tensor")
    space_count = lax.axis_size("space")
    image_total = features.shape[0] * lax.axis_size("dp")
    col_count = features.shape[2]
    chan_total = features.shape[3]
    height = features.shape[1] * tensor_count * space_count
    scale = 1.0 / math.sqrt(height * col_count * chan_total)
    gweight = r1_factor / image_total
    local_maps = lax.all_to_all(features, "tensor", split_axis=3, concat_axis=1, tiled=True)
    x_pad = pad_cols(padded_2(local_maps, (("space", 1),), 1))
    kernel_cols = lax.all_to_all(kernel, "tensor", split_axis=3, concat_axis=2, tiled=True)
    hidden = forward_conv(x_pad, kernel_cols)
    class_count = embedding.shape[0]
    onehot = (labels[:, None] == jnp.arange(class_count, dtype=jnp.int32)[None, :]).astype(
        jnp.float32
    )
    embed_rows = jnp.dot(onehot, embedding, precision=lax.Precision.HIGHEST)
    embed_four = embed_rows[:, None, None, :]
    sig = jax.nn.sigmoid(hidden)
    act = hidden * sig
    slope = sig * (1.0 + hidden * (1.0 - sig))
    curve = sig * (1.0 - sig) * (2.0 + hidden * (1.0 - 2.0 * sig))
    score = lax.psum(scale * jnp.sum(act * embed_four, axis=(1, 2, 3)), ("space", "tensor"))
    coeff = -jax.nn.sigmoid(-score) / image_total
    grad_hidden = (embed_four * slope * scale).astype(jnp.bfloat16)
    gh_pad = pad_cols(padded_2(grad_hidden, (("space", 1),), 1))
    flipped = jnp.transpose(kernel[::-1, ::-1], (0, 1, 3, 2))
    gh_whole = lax.all_gather(gh_pad, "tensor", axis=3, tiled=True)
    grad_input = conv_valid(gh_whole, flipped).astype(jnp.bfloat16)
    gx_pad = pad_cols(padded_2(grad_input, (("space", 1),), 1))
    direct = taps_of(gx_pad, gh_whole[:, 1:-1, 1:-1, :])
    second = forward_conv(gx_pad, kernel_cols)
    pre = (
        coeff[:, None, None, None] * embed_four * slope * scale
        + gweight * second * embed_four * curve * scale
    ).astype(jnp.bfloat16)
    adversarial = taps_of(x_pad, lax.all_gather(pre, "tensor", axis=3, tiled=True))
    wgrad = adversarial + gweight * direct
    per_image = coeff[:, None] * scale * jnp.sum(act, axis=(1, 2)) + gweight * scale * jnp.sum(
        second * slope, axis=(1, 2)
    )
    egrad = jnp.dot(onehot.T, per_image, precision=lax.Precision.HIGHEST)
    wtotal, etotal = lax.psum((wgrad, egrad), ("dp", "space"))
    return (wtotal, etotal)


def solution(mesh):
    placed = (
        P("dp", ("space", "tensor"), None, None),
        P(None, None, "tensor", None),
        P(None, "tensor"),
        P("dp"),
    )
    return jax.shard_map(
        body,
        mesh=mesh,
        in_specs=placed,
        out_specs=(P(None, None, "tensor", None), P(None, "tensor")),
        check_vma=False,
    )
```

profile of v0, /device:TPU:1, one launch (start us, length us, event | category | flops | bytes accessed | tf_op | source)
XLA Modules:
  0.0 670.4 jit_solution(11944661111741566787)
XLA Ops:
  7.2 2.1 copy.31
  9.3 1.4 reshape.249
  10.8 12.3 %all_to_all.36 = bf16[8,2,8192]{2,1,0:T(2,128)(2,1)S(1)} all-to-all(bf16[8,2,8192]{2,1,0:T(2,128)(2,1)S(1)} %reshape.249), channel_id=1, replica_groups=mesh['dp'=4,'space'=8,'tensor'=8] {'tensor'}, dimensions={0} | all-to-all | bytes 524288 | tf_op jit(solution)/shard_map/all_to_all | solution.py:72
  23.0 1.2 reshape.250
  24.2 1.2 copy.32
  25.5 1.3 collective-permute-start.1
  26.8 9.4 %collective-permute-start = (bf16[1,1,64,128]{3,2,1,0:T(8,128)(2,1)S(1)}, bf16[1,1,64,128]{3,2,1,0:T(8,128)(2,1)S(1)}, u32[]{:S(2)}, u32[]{:S(2)}) collective-permute-start(bf16[1,1,64,128]{3,2,1,0:T(8,128)(2,1)S(1)} %get-tuple-element.11), channel_id=1, source_target_pairs={{0,8},{8,16},{16,24},{24,32},{32,40},{40,48},{48,56},{1,9},{9,17},... | collective-permute-start | bytes 49160 | tf_op jit(solution)/shard_map/ppermute | solution.py:15
  36.2 0.8 collective-permute-done
  37.1 0.8 select_maximum_fusion.4
  37.9 3.6 copy.36
  41.5 6.2 all-to-all-start.1
  48.7 47.4 %all-to-all-done.1 = bf16[3,3,128,1024]{2,1,0,3:T(4,128)(2,1)} async-done(((bf16[3,3,128,1024]{2,1,0,3:T(4,128)(2,1)}), bf16[3,3,128,1024]{2,1,0,3:T(4,128)(2,1)}, u32[]{:S(2)}, u32[]{:S(2)}) %all-to-all-start.1) | async-done | bytes 2359328 | tf_op jit(solution)/shard_map/all_to_all | solution.py:74
  96.1 5.6 copy.37
  101.7 3.2 copy.60
  104.9 0.6 pad.13.clone
  105.5 1.5 copy.35
  107.2 6.5 multiply_convert_fusion
  113.8 1.3 collective-permute-start.3
  115.1 9.5 %collective-permute-start.2 = (bf16[1,1,64,128]{3,2,1,0:T(8,128)(2,1)S(1)}, bf16[1,1,64,128]{3,2,1,0:T(8,128)(2,1)S(1)}, u32[]{:S(2)}, u32[]{:S(2)}) collective-permute-start(bf16[1,1,64,128]{3,2,1,0:T(8,128)(2,1)S(1)} %slice.123), channel_id=1, source_target_pairs={{0,8},{8,16},{16,24},{24,32},{32,40},{40,48},{48,56},{1,9},{9,17},... | collective-permute-start | bytes 49160 | tf_op jit(solution)/shard_map/ppermute | solution.py:15
  125.1 0.8 select_maximum_fusion.2
  126.0 39.5 %all-gather.8.cloned.1.call-done = bf16[1,18,66,1024]{3,2,1,0:T(8,128)(2,1)} async-done(((bf16[1,18,66,128]{3,2,1,0:T(8,128)(2,1)}), bf16[1,18,66,1024]{3,2,1,0:T(8,128)(2,1)}) %all-gather.8.cloned.1.call-update) | async-done | bytes 2433040 | tf_op jit(solution)/shard_map/all_gather | solution.py:91
  165.5 3.2 copy.61
  168.6 0.6 pad.15.clone
  169.2 1.5 copy.44
  170.8 5.7 fusion.81
  176.6 1.3 collective-permute-start.5
  178.0 8.0 %collective-permute-start.4 = (bf16[1,1,64,128]{3,2,1,0:T(8,128)(2,1)S(1)}, bf16[1,1,64,128]{3,2,1,0:T(8,128)(2,1)S(1)}, u32[]{:S(2)}, u32[]{:S(2)}) collective-permute-start(bf16[1,1,64,128]{3,2,1,0:T(8,128)(2,1)S(1)} %slice.129), channel_id=1, source_target_pairs={{0,8},{8,16},{16,24},{24,32},{32,40},{40,48},{48,56},{1,9},{9,17},... | collective-permute-start | bytes 49160 | tf_op jit(solution)/shard_map/ppermute | solution.py:15
  186.1 0.7 copy-done.14
  186.9 0.8 select_maximum_fusion
  188.0 36.1 %all-gather.10.cloned.1.call-done = bf16[1,18,66,1024]{3,2,1,0:T(8,128)(2,1)} async-done(((bf16[1,18,66,128]{3,2,1,0:T(8,128)(2,1)}), bf16[1,18,66,1024]{3,2,1,0:T(8,128)(2,1)}) %all-gather.10.cloned.1.call-update) | async-done | bytes 2433040 | tf_op jit(solution)/shard_map/all_gather | solution.py:59
  224.0 3.2 copy.62
  227.2 0.6 pad.17.clone
  227.8 1.5 copy.51
  229.6 7.2 %select_reduce_fusion.2 = (f32[128]{0:T(128)S(1)}, f32[128]{0:T(128)S(1)}, f32[]{:T(128)}, f32[16,8,9,128]{3,1,2,0:T(8,128)}) fusion(pred[8,9]{0,1:T(8,128)(4,1)S(1)} %copy-done.17, f32[16,8,9,128]{3,1,2,0:T(8,128)S(1)} %copy-done.15, f32[128]{0:T(128)S(1)} %convolution_bitcast_fusion.9, bf16[3,3,1024,128]{3,2,1,0:T(8,128)(2,1)S(1)} %bitcast.242, ...), kind=kOutput, calls=%fused_computation.90 | convolution fusion | flops 2730147840 | bytes 6710860 | tf_op jit(solution)/shard_map/conv_general_dilated | solution.py:24
  237.5 201.6 %psum.21 = f32[1]{0:T(128)} all-reduce(f32[1]{0:T(128)} %bitcast.13), channel_id=1, replica_groups=mesh['dp'=4,'space'=8,'tensor'=8] {'space','tensor'}, use_global_device_ids=true, to_apply=%region_1.2 | all-reduce | flops 1 | bytes 8 | tf_op jit(solution)/shard_map/psum | solution.py:86
  439.8 1.7 fusion.91
  441.5 0.8 copy.59
  442.6 1.8 convolution_bitcast_fusion.4
  444.4 1.8 convolution_bitcast_fusion.1
  446.2 0.8 convolution_bitcast_fusion
  447.1 0.8 convolution_bitcast_fusion.2
  448.1 1.6 copy-done.7
  449.6 0.8 convolution_bitcast_fusion.7
  450.4 0.8 convolution_bitcast_fusion.6
  451.3 0.8 convolution_bitcast_fusion.8
  452.1 0.8 convolution_bitcast_fusion.3
  452.9 0.8 convolution_bitcast_fusion.5
  453.7 1.9 maximum_bitcast_fusion.3
  455.6 1.0 broadcast_multiply_fusion
  456.6 16.8 %all-gather.12.cloned.1.call-done = bf16[16,1,64,1024]{3,2,0,1:T(8,128)(2,1)} async-done(((bf16[16,1,64,128]{3,2,0,1:T(8,128)(2,1)}), bf16[16,1,64,1024]{3,2,0,1:T(8,128)(2,1)}) %all-gather.12.cloned.1.call-update) | async-done | bytes 2097168 | tf_op jit(solution)/shard_map/all_gather | solution.py:100
  473.4 2.2 fusion.69
  476.1 0.5 fusion.63
  476.8 0.5 fusion.51
  477.3 0.5 fusion.48
  477.8 0.5 fusion.45
  478.2 0.5 fusion.60
  478.7 0.5 fusion.54
  479.2 0.5 fusion.57
  480.0 1.1 copy-done.4
  481.1 0.5 copy-done.5
  481.6 2.7 maximum_add_fusion
  484.3 173.2 %all-reduce.6.cloned.1.call-done = (f32[3,3,128,1024]{3,2,1,0:T(8,128)}, f32[1000,128]{1,0:T(8,128)}) async-done(((f32[3,3,128,1024]{3,2,1,0:T(8,128)}, f32[1000,128]{1,0:T(8,128)}), (f32[3,3,128,1024]{3,2,1,0:T(8,128)}, f32[1000,128]{1,0:T(8,128)})) %all-reduce.6.cloned.1.call-update) | async-done | bytes 5230608 | tf_op jit(solution)/shard_map/psum | solution.py:106
  657.5 5.3 copy.74
  662.8 0.8 copy.75
  (84 shorter events, 3.4 us)
Async XLA Ops:
  7.2 41.3 %copy-start = (f32[1000,128]{1,0:T(8,128)S(1)}, f32[1000,128]{1,0:T(8,128)}, u32[]{:S(2)}) copy-start(f32[1000,128]{1,0:T(8,128)} %param.6) | copy-start | bytes 1536004
  7.2 30.7 %copy-start.8 = (bf16[3,3,128,1024]{3,2,1,0:T(8,128)(2,1)S(1)}, bf16[3,3,128,1024]{3,2,1,0:T(8,128)(2,1)}, u32[]{:S(2)}) copy-start(bf16[3,3,128,1024]{3,2,1,0:T(8,128)(2,1)} %param.5) | copy-start | bytes 7077892
  7.2 94.5 %all-gather.6.cloned.1.call-start = ((), (), s32[]{:S(2)}) async-start(), calls=%async_computation.2 | async-start | bytes 2985984 | tf_op jit(solution)/shard_map/all_gather | solution.py:59
  25.5 10.8 %collective-permute-start.1 = (bf16[1,1,64,128]{3,2,1,0:T(8,128)(2,1)S(1)}, bf16[1,1,64,128]{3,2,1,0:T(8,128)(2,1)S(1)}, u32[]{:S(2)}, u32[]{:S(2)}) collective-permute-start(bf16[1,1,64,128]{3,2,1,0:T(8,128)(2,1)S(1)} %get-tuple-element.12), channel_id=1, source_target_pairs={{8,0},{16,8},{24,16},{32,24},{40,32},{48,40},{56,48},{9,1},{17,9},... | collective-permute-start | bytes 49160 | tf_op jit(solution)/shard_map/ppermute | solution.py:18
  26.8 10.3 %collective-permute-start = (bf16[1,1,64,128]{3,2,1,0:T(8,128)(2,1)S(1)}, bf16[1,1,64,128]{3,2,1,0:T(8,128)(2,1)S(1)}, u32[]{:S(2)}, u32[]{:S(2)}) collective-permute-start(bf16[1,1,64,128]{3,2,1,0:T(8,128)(2,1)S(1)} %get-tuple-element.11), channel_id=1, source_target_pairs={{0,8},{8,16},{16,24},{24,32},{32,40},{40,48},{48,56},{1,9},{9,17},... | collective-permute-start | bytes 49160 | tf_op jit(solution)/shard_map/ppermute | solution.py:15
  41.5 54.6 %all-to-all-start.1 = ((bf16[3,3,128,1024]{2,1,0,3:T(4,128)(2,1)}), bf16[3,3,128,1024]{2,1,0,3:T(4,128)(2,1)}, u32[]{:S(2)}, u32[]{:S(2)}) async-start(bf16[3,3,128,1024]{2,1,0,3:T(4,128)(2,1)} %copy.36), calls=%async_computation.1 | async-start | bytes 6291456 | tf_op jit(solution)/shard_map/all_to_all | solution.py:74
  47.8 117.7 %all-gather.8.cloned.1.call-start = ((), (), s32[]{:S(2)}) async-start(), calls=%async_computation.3 | async-start | bytes 2985984 | tf_op jit(solution)/shard_map/all_gather | solution.py:91
  105.5 1.7 copy-start.9
  105.5 1.7 copy-start.17
  113.8 11.1 %collective-permute-start.3 = (bf16[1,1,64,128]{3,2,1,0:T(8,128)(2,1)S(1)}, bf16[1,1,64,128]{3,2,1,0:T(8,128)(2,1)S(1)}, u32[]{:S(2)}, u32[]{:S(2)}) collective-permute-start(bf16[1,1,64,128]{3,2,1,0:T(8,128)(2,1)S(1)} %slice.126), channel_id=1, source_target_pairs={{8,0},{16,8},{24,16},{32,24},{40,32},{48,40},{56,48},{9,1},{17,9},... | collective-permute-start | bytes 49160 | tf_op jit(solution)/shard_map/ppermute | solution.py:18
  115.1 9.9 %collective-permute-start.2 = (bf16[1,1,64,128]{3,2,1,0:T(8,128)(2,1)S(1)}, bf16[1,1,64,128]{3,2,1,0:T(8,128)(2,1)S(1)}, u32[]{:S(2)}, u32[]{:S(2)}) collective-permute-start(bf16[1,1,64,128]{3,2,1,0:T(8,128)(2,1)S(1)} %slice.123), channel_id=1, source_target_pairs={{0,8},{8,16},{16,24},{24,32},{32,40},{40,48},{48,56},{1,9},{9,17},... | collective-permute-start | bytes 49160 | tf_op jit(solution)/shard_map/ppermute | solution.py:15
  125.9 98.1 %all-gather.10.cloned.1.call-start = ((), (), s32[]{:S(2)}) async-start(), calls=%async_computation.4 | async-start | bytes 2985984 | tf_op jit(solution)/shard_map/all_gather | solution.py:59
  176.6 10.2 %collective-permute-start.5 = (bf16[1,1,64,128]{3,2,1,0:T(8,128)(2,1)S(1)}, bf16[1,1,64,128]{3,2,1,0:T(8,128)(2,1)S(1)}, u32[]{:S(2)}, u32[]{:S(2)}) collective-permute-start(bf16[1,1,64,128]{3,2,1,0:T(8,128)(2,1)S(1)} %slice.132), channel_id=1, source_target_pairs={{8,0},{16,8},{24,16},{32,24},{40,32},{48,40},{56,48},{9,1},{17,9},... | collective-permute-start | bytes 49160 | tf_op jit(solution)/shard_map/ppermute | solution.py:18
  178.0 8.9 %collective-permute-start.4 = (bf16[1,1,64,128]{3,2,1,0:T(8,128)(2,1)S(1)}, bf16[1,1,64,128]{3,2,1,0:T(8,128)(2,1)S(1)}, u32[]{:S(2)}, u32[]{:S(2)}) collective-permute-start(bf16[1,1,64,128]{3,2,1,0:T(8,128)(2,1)S(1)} %slice.129), channel_id=1, source_target_pairs={{0,8},{8,16},{16,24},{24,32},{32,40},{40,48},{48,56},{1,9},{9,17},... | collective-permute-start | bytes 49160 | tf_op jit(solution)/shard_map/ppermute | solution.py:15
  186.0 0.7 copy-start.14
  186.8 40.4 %copy-start.12 = (bf16[16,1,64,128]{3,2,0,1:T(8,128)(2,1)}, bf16[16,1,64,128]{3,2,0,1:T(8,128)(2,1)S(1)}, u32[]{:S(2)}) copy-start(bf16[16,1,64,128]{3,2,0,1:T(8,128)(2,1)S(1)} %copy.70) | copy-start | bytes 786436
  187.7 285.7 %all-gather.12.cloned.1.call-start = ((), (), s32[]{:S(2)}) async-start(), calls=%async_computation.5 | async-start | bytes 2359296 | tf_op jit(solution)/shard_map/all_gather | solution.py:100
  227.8 1.7 copy-start.10
  227.8 1.8 copy-start.15
  236.8 205.8 %copy-start.6 = (bf16[1,18,66,1024]{3,2,1,0:T(8,128)(2,1)S(1)}, bf16[1,18,66,1024]{3,2,1,0:T(8,128)(2,1)}, u32[]{:S(2)}) copy-start(bf16[1,18,66,1024]{3,2,1,0:T(8,128)(2,1)} %all-gather.8.cloned.1.call-done) | copy-start | bytes 7299076
  442.4 215.2 %all-reduce.6.cloned.1.call-start = ((), (), s32[]{:S(2)}) async-start(), calls=%async_computation.6 | async-start | bytes 10461184 | tf_op jit(solution)/shard_map/psum | solution.py:106
  444.4 1.8 copy-start.11
  447.9 1.8 copy-start.7
  447.9 1.7 copy-start.13
  453.7 19.7 %copy-start.3 = (bf16[1,18,66,128]{3,2,1,0:T(8,128)(2,1)S(1)}, bf16[1,18,66,128]{3,2,1,0:T(8,128)(2,1)}, u32[]{:S(2)}) copy-start(bf16[1,18,66,128]{3,2,1,0:T(8,128)(2,1)} %select_maximum_fusion.4) | copy-start | bytes 912388
  473.4 2.2 copy-start.2
  479.7 1.4 copy-start.4
  479.7 1.9 copy-start.5
  657.5 5.3 copy-start.16
  657.5 6.1 copy-start.1
Sparse Core Ops, SparseCore 0:
  38.0 50.9 all-gather.5
  126.0 39.3 all-gather.7
  187.8 36.1 all-gather.9
  442.5 30.9 all-gather.11
  484.4 173.0 all-reduce.5
where the time goes:
time: 679 us; the launch traced here: 670 us
  waiting for transfers between devices  314 us (46%)
  blocking collectives  214 us (32%)
  local copies, waits for them, and re-layouts  42.6 us (6%)
  starting transfers between devices  37.6 us (6%)
  matrix products  35 us (5%)
  between operations  16.7 us (2%)
  other arithmetic  10.4 us (2%)
    psum x1, blocking collectives, body(): lax.psum(scale * jnp.sum(act * embed_four, axis=(1, 2, 3)), ('space', 'te...  202 us
    psum x1, waiting for transfers between devices, body(): wtotal, etotal = lax.psum((wgrad, egrad), ('dp', 'space'))  173 us
    all_to_all x1, waiting for transfers between devices, body(): lax.all_to_all(kernel, 'tensor', split_axis=3, concat_axis=2, tiled=True)  47.4 us
    all_gather x1, waiting for transfers between devices, body(): gh_whole = lax.all_gather(gh_pad, 'tensor', axis=3, tiled=True)  39.5 us
    all_gather x2, waiting for transfers between devices, forward_conv(): whole = lax.all_gather(padded, 'tensor', axis=3, tiled=True)  36.1 us
    unnamed x48, local copies, waits for them, and re-layouts  28.9 us
    ppermute x3, starting transfers between devices, padded_2(): lax.ppermute(lax.slice_in_dim(block, block.shape[dim] - width, None, axis...  27 us
    conv_general_dilated x3, matrix products, conv_valid(): lax.conv_general_dilated(padded, kern, (1, 1), 'VALID', dimension_numbers...  19.5 us
  transfers between devices with their start and end apart: 12, of which 7 were waited for; matrix products, arithmetic and copies ran while one was open for 3% of the time, Pallas kernels for 0%

commit v1 on v0

--- a/solution.py
+++ b/solution.py
@@ -83,7 +83,7 @@
     act = hidden * sig
     slope = sig * (1.0 + hidden * (1.0 - sig))
     curve = sig * (1.0 - sig) * (2.0 + hidden * (1.0 - 2.0 * sig))
-    score = lax.psum(scale * jnp.sum(act * embed_four, axis=(1, 2, 3)), ("space", "tensor"))
+    score = lax.psum(lax.psum(scale * jnp.sum(act * embed_four, axis=(1, 2, 3)), "space"), "tensor")
     coeff = -jax.nn.sigmoid(-score) / image_total
     grad_hidden = (embed_four * slope * scale).astype(jnp.bfloat16)
     gh_pad = pad_cols(padded_2(grad_hidden, (("space", 1),), 1))

time: 679 us -> 515 us (0.76)
  blocking collectives: 214 us -> 57.9 us
  waiting for transfers between devices: 314 us -> 305 us
    psum x1 -> x2, blocking collectives: 202 us -> 45.7 us  [the longest x1 29.3 us: body(): lax.psum(scale * jnp.sum(act * embed_four, axis=(1, 2, 3)), 'space')]
    all_gather x1, waiting for transfers between devices: 16.8 us -> 7.63 us  [body(): lax.all_gather(pre, 'tensor', axis=3, tiled=True)]
  transfers between devices with their start and end apart: 12 -> 12, of which waited for: 7 -> 7; matrix products, arithmetic and copies ran while one was open for 3% -> 4% of each run, Pallas kernels for 0% -> 0%
where the time goes in v1:
time: 515 us; the launch traced here: 506 us
  waiting for transfers between devices  305 us (59%)
  blocking collectives  57.9 us (11%)
  local copies, waits for them, and re-layouts  42.6 us (8%)
  starting transfers between devices  37.6 us (7%)
  matrix products  35.1 us (7%)
  between operations  16.9 us (3%)
  other arithmetic  10.4 us (2%)
    psum x1, waiting for transfers between devices, body(): wtotal, etotal = lax.psum((wgrad, egrad), ('dp', 'space'))  173 us
    all_to_all x1, waiting for transfers between devices, body(): lax.all_to_all(kernel, 'tensor', split_axis=3, concat_axis=2, tiled=True)  47.4 us
    all_gather x1, waiting for transfers between devices, body(): gh_whole = lax.all_gather(gh_pad, 'tensor', axis=3, tiled=True)  39.5 us
    all_gather x2, waiting for transfers between devices, forward_conv(): whole = lax.all_gather(padded, 'tensor', axis=3, tiled=True)  36.1 us
    psum x1, blocking collectives, body(): lax.psum(scale * jnp.sum(act * embed_four, axis=(1, 2, 3)), 'space')  29.3 us
    unnamed x48, local copies, waits for them, and re-layouts  28.9 us
    ppermute x3, starting transfers between devices, padded_2(): lax.ppermute(lax.slice_in_dim(block, block.shape[dim] - width, None, axis...  27 us
    conv_general_dilated x3, matrix products, conv_valid(): lax.conv_general_dilated(padded, kern, (1, 1), 'VALID', dimension_numbers...  19.5 us
  transfers between devices with their start and end apart: 12, of which 7 were waited for; matrix products, arithmetic and copies ran while one was open for 4% of the time, Pallas kernels for 0%

profile of v1, /device:TPU:1, one launch (start us, length us, event | category | flops | bytes accessed | tf_op | source)
XLA Modules:
  0.0 505.6 jit_solution(9089792489574850799)
XLA Ops:
  7.2 2.1 copy.31
  9.3 1.4 reshape.249
  10.8 12.3 %all_to_all.36 = bf16[8,2,8192]{2,1,0:T(2,128)(2,1)S(1)} all-to-all(bf16[8,2,8192]{2,1,0:T(2,128)(2,1)S(1)} %reshape.249), channel_id=1, replica_groups=mesh['dp'=4,'space'=8,'tensor'=8] {'tensor'}, dimensions={0} | all-to-all | bytes 524288 | tf_op jit(solution)/shard_map/all_to_all | solution.py:72
  23.0 1.2 reshape.250
  24.2 1.2 copy.32
  25.5 1.3 collective-permute-start.1
  26.8 9.4 %collective-permute-start = (bf16[1,1,64,128]{3,2,1,0:T(8,128)(2,1)S(1)}, bf16[1,1,64,128]{3,2,1,0:T(8,128)(2,1)S(1)}, u32[]{:S(2)}, u32[]{:S(2)}) collective-permute-start(bf16[1,1,64,128]{3,2,1,0:T(8,128)(2,1)S(1)} %get-tuple-element.11), channel_id=1, source_target_pairs={{0,8},{8,16},{16,24},{24,32},{32,40},{40,48},{48,56},{1,9},{9,17},... | collective-permute-start | bytes 49160 | tf_op jit(solution)/shard_map/ppermute | solution.py:15
  36.2 0.8 collective-permute-done
  37.1 0.8 select_maximum_fusion.4
  37.9 3.6 copy.36
  41.5 6.2 %all-to-all-start.1 = ((bf16[3,3,128,1024]{2,1,0,3:T(4,128)(2,1)}), bf16[3,3,128,1024]{2,1,0,3:T(4,128)(2,1)}, u32[]{:S(2)}, u32[]{:S(2)}) async-start(bf16[3,3,128,1024]{2,1,0,3:T(4,128)(2,1)} %copy.36), calls=%async_computation.1 | async-start | bytes 6291456 | tf_op jit(solution)/shard_map/all_to_all | solution.py:74
  48.7 47.4 %all-to-all-done.1 = bf16[3,3,128,1024]{2,1,0,3:T(4,128)(2,1)} async-done(((bf16[3,3,128,1024]{2,1,0,3:T(4,128)(2,1)}), bf16[3,3,128,1024]{2,1,0,3:T(4,128)(2,1)}, u32[]{:S(2)}, u32[]{:S(2)}) %all-to-all-start.1) | async-done | bytes 2359328 | tf_op jit(solution)/shard_map/all_to_all | solution.py:74
  96.1 5.6 %copy.37 = bf16[3,3,128,8,128]{4,2,3,1,0:T(8,128)(2,1)} copy(bf16[3,3,128,8,128]{2,1,0,4,3:T(4,128)(2,1)} %bitcast.8) | data formatting | bytes 4718592 | tf_op jit(solution)/shard_map/all_to_all | solution.py:74
  101.7 3.2 copy.60
  104.9 0.6 pad.13.clone
  105.5 1.5 copy.35
  107.2 6.5 %multiply_convert_fusion = (bf16[16,8,9,128]{3,1,2,0:T(8,128)(2,1)S(1)}, f32[16,8,9,128]{3,1,2,0:T(8,128)}) fusion(f32[128]{0:T(128)S(1)} %convolution_bitcast_fusion.9, bf16[3,3,1024,128]{3,2,1,0:T(8,128)(2,1)S(1)} %bitcast.241, bf16[18,1,7,2,1024]{4,2,3,0,1:T(8,128)(2,1)S(1)} %slice.121, bf16[18,1,8,9,1024]{4,2,3,0,1:T(8,128)(2,1)S(1)} %copy.35, ...), kind=kOutput, calls=%fused_computation.88 | convolution fusion | flops 2729263104 | bytes 6414920 | tf_op jit(solution)/shard_map/conv_general_dilated | solution.py:24
  113.8 1.3 collective-permute-start.3
  115.1 9.5 %collective-permute-start.2 = (bf16[1,1,64,128]{3,2,1,0:T(8,128)(2,1)S(1)}, bf16[1,1,64,128]{3,2,1,0:T(8,128)(2,1)S(1)}, u32[]{:S(2)}, u32[]{:S(2)}) collective-permute-start(bf16[1,1,64,128]{3,2,1,0:T(8,128)(2,1)S(1)} %slice.123), channel_id=1, source_target_pairs={{0,8},{8,16},{16,24},{24,32},{32,40},{40,48},{48,56},{1,9},{9,17},... | collective-permute-start | bytes 49160 | tf_op jit(solution)/shard_map/ppermute | solution.py:15
  125.0 0.8 select_maximum_fusion.2
  125.9 39.5 %all-gather.8.cloned.1.call-done = bf16[1,18,66,1024]{3,2,1,0:T(8,128)(2,1)} async-done(((bf16[1,18,66,128]{3,2,1,0:T(8,128)(2,1)}), bf16[1,18,66,1024]{3,2,1,0:T(8,128)(2,1)}) %all-gather.8.cloned.1.call-update) | async-done | bytes 2433040 | tf_op jit(solution)/shard_map/all_gather | solution.py:91
  165.5 3.2 copy.61
  168.6 0.6 pad.15.clone
  169.2 1.5 copy.44
  170.8 5.7 %fusion.81 = bf16[16,8,9,128]{3,1,2,0:T(8,128)(2,1)S(1)} fusion(bf16[3,3,128,1024]{3,2,1,0:T(8,128)(2,1)S(1)} %copy-done.8, bf16[18,1,7,2,1024]{4,2,3,0,1:T(8,128)(2,1)S(1)} %slice.127, bf16[18,1,8,9,1024]{4,2,3,0,1:T(8,128)(2,1)S(1)} %copy.44, pred[8,9]{0,1:T(8,128)(4,1)S(1)} %copy-done.17), kind=kOutput, calls=%fused_computation.73 | convolution fusion | flops 2727936000 | bytes 5824584 | tf_op jit(solution)/shard_map/conv_general_dilated | solution.py:24
  176.6 1.3 collective-permute-start.5
  178.0 8.0 %collective-permute-start.4 = (bf16[1,1,64,128]{3,2,1,0:T(8,128)(2,1)S(1)}, bf16[1,1,64,128]{3,2,1,0:T(8,128)(2,1)S(1)}, u32[]{:S(2)}, u32[]{:S(2)}) collective-permute-start(bf16[1,1,64,128]{3,2,1,0:T(8,128)(2,1)S(1)} %slice.129), channel_id=1, source_target_pairs={{0,8},{8,16},{16,24},{24,32},{32,40},{40,48},{48,56},{1,9},{9,17},... | collective-permute-start | bytes 49160 | tf_op jit(solution)/shard_map/ppermute | solution.py:15
  186.0 0.7 copy-done.14
  186.9 0.8 select_maximum_fusion
  187.9 36.1 %all-gather.10.cloned.1.call-done = bf16[1,18,66,1024]{3,2,1,0:T(8,128)(2,1)} async-done(((bf16[1,18,66,128]{3,2,1,0:T(8,128)(2,1)}), bf16[1,18,66,1024]{3,2,1,0:T(8,128)(2,1)}) %all-gather.10.cloned.1.call-update) | async-done | bytes 2433040 | tf_op jit(solution)/shard_map/all_gather | solution.py:59
  224.0 3.2 copy.62
  227.2 0.6 pad.17.clone
  227.8 1.5 copy.51
  229.6 7.3 %select_reduce_fusion.2 = (f32[128]{0:T(128)S(1)}, f32[128]{0:T(128)S(1)}, f32[]{:T(128)}, f32[16,8,9,128]{3,1,2,0:T(8,128)}) fusion(pred[8,9]{0,1:T(8,128)(4,1)S(1)} %copy-done.17, f32[16,8,9,128]{3,1,2,0:T(8,128)S(1)} %copy-done.15, f32[128]{0:T(128)S(1)} %convolution_bitcast_fusion.9, bf16[3,3,1024,128]{3,2,1,0:T(8,128)(2,1)S(1)} %bitcast.242, ...), kind=kOutput, calls=%fused_computation.90 | convolution fusion | flops 2730147840 | bytes 6710860 | tf_op jit(solution)/shard_map/conv_general_dilated | solution.py:24
  237.7 29.3 %psum.28 = f32[1]{0:T(128)} all-reduce(f32[1]{0:T(128)} %bitcast.13), channel_id=1, replica_groups=mesh['dp'=4,'space'=8,'tensor'=8] {'space'}, use_global_device_ids=true, to_apply=%region_1.2 | all-reduce | flops 1 | bytes 8 | tf_op jit(solution)/shard_map/psum | solution.py:86
  267.0 16.4 %psum.29 = f32[1]{0:T(128)} all-reduce(f32[1]{0:T(128)} %psum.28), channel_id=1, replica_groups=mesh['dp'=4,'space'=8,'tensor'=8] {'tensor'}, use_global_device_ids=true, to_apply=%region_2.3 | all-reduce | flops 1 | bytes 8 | tf_op jit(solution)/shard_map/psum | solution.py:86
  284.1 1.7 fusion.91
  285.9 0.8 copy.59
  286.9 1.8 convolution_bitcast_fusion.4
  288.7 1.8 convolution_bitcast_fusion.1
  290.5 0.8 convolution_bitcast_fusion
  291.4 0.8 convolution_bitcast_fusion.2
  292.4 1.6 copy-done.7
  293.9 0.8 convolution_bitcast_fusion.7
  294.7 0.8 convolution_bitcast_fusion.6
  295.6 0.8 convolution_bitcast_fusion.8
  296.4 0.8 convolution_bitcast_fusion.3
  297.2 0.8 convolution_bitcast_fusion.5
  298.0 1.9 maximum_bitcast_fusion.3
  300.0 1.0 broadcast_multiply_fusion
  300.9 7.6 %all-gather.12.cloned.1.call-done = bf16[16,1,64,1024]{3,2,0,1:T(8,128)(2,1)} async-done(((bf16[16,1,64,128]{3,2,0,1:T(8,128)(2,1)}), bf16[16,1,64,1024]{3,2,0,1:T(8,128)(2,1)}) %all-gather.12.cloned.1.call-update) | async-done | bytes 2097168 | tf_op jit(solution)/shard_map/all_gather | solution.py:100
  308.6 2.2 fusion.69
  310.8 0.5 fusion.66
  311.3 0.5 fusion.63
  311.9 0.5 fusion.51
  313.4 0.5 fusion.60
  313.8 0.5 fusion.54
  314.3 0.5 fusion.57
  315.1 1.1 copy-done.4
  316.2 0.5 copy-done.5
  316.7 2.7 maximum_add_fusion
  319.4 173.3 %all-reduce.6.cloned.1.call-done = (f32[3,3,128,1024]{3,2,1,0:T(8,128)}, f32[1000,128]{1,0:T(8,128)}) async-done(((f32[3,3,128,1024]{3,2,1,0:T(8,128)}, f32[1000,128]{1,0:T(8,128)}), (f32[3,3,128,1024]{3,2,1,0:T(8,128)}, f32[1000,128]{1,0:T(8,128)})) %all-reduce.6.cloned.1.call-update) | async-done | bytes 5230608 | tf_op jit(solution)/shard_map/psum | solution.py:106
  492.7 5.3 %copy.74 = f32[3,3,128,1024]{3,2,1,0:T(8,128)} copy(f32[3,3,128,1024]{3,2,1,0:T(8,128)} %get-tuple-element.22) | data formatting | bytes 9437184
  498.1 0.8 copy.75
  (85 shorter events, 3.9 us)
Async XLA Ops:
  7.2 41.3 %copy-start = (f32[1000,128]{1,0:T(8,128)S(1)}, f32[1000,128]{1,0:T(8,128)}, u32[]{:S(2)}) copy-start(f32[1000,128]{1,0:T(8,128)} %param.6) | copy-start | bytes 1536004
  7.2 30.7 %copy-start.8 = (bf16[3,3,128,1024]{3,2,1,0:T(8,128)(2,1)S(1)}, bf16[3,3,128,1024]{3,2,1,0:T(8,128)(2,1)}, u32[]{:S(2)}) copy-start(bf16[3,3,128,1024]{3,2,1,0:T(8,128)(2,1)} %param.5) | copy-start | bytes 7077892
  7.2 94.5 %all-gather.6.cloned.1.call-start = ((), (), s32[]{:S(2)}) async-start(), calls=%async_computation.2 | async-start | bytes 2985984 | tf_op jit(solution)/shard_map/all_gather | solution.py:59
  25.5 10.8 %collective-permute-start.1 = (bf16[1,1,64,128]{3,2,1,0:T(8,128)(2,1)S(1)}, bf16[1,1,64,128]{3,2,1,0:T(8,128)(2,1)S(1)}, u32[]{:S(2)}, u32[]{:S(2)}) collective-permute-start(bf16[1,1,64,128]{3,2,1,0:T(8,128)(2,1)S(1)} %get-tuple-element.12), channel_id=1, source_target_pairs={{8,0},{16,8},{24,16},{32,24},{40,32},{48,40},{56,48},{9,1},{17,9},... | collective-permute-start | bytes 49160 | tf_op jit(solution)/shard_map/ppermute | solution.py:18
  26.8 10.3 %collective-permute-start = (bf16[1,1,64,128]{3,2,1,0:T(8,128)(2,1)S(1)}, bf16[1,1,64,128]{3,2,1,0:T(8,128)(2,1)S(1)}, u32[]{:S(2)}, u32[]{:S(2)}) collective-permute-start(bf16[1,1,64,128]{3,2,1,0:T(8,128)(2,1)S(1)} %get-tuple-element.11), channel_id=1, source_target_pairs={{0,8},{8,16},{16,24},{24,32},{32,40},{40,48},{48,56},{1,9},{9,17},... | collective-permute-start | bytes 49160 | tf_op jit(solution)/shard_map/ppermute | solution.py:15
  41.5 54.6 %all-to-all-start.1 = ((bf16[3,3,128,1024]{2,1,0,3:T(4,128)(2,1)}), bf16[3,3,128,1024]{2,1,0,3:T(4,128)(2,1)}, u32[]{:S(2)}, u32[]{:S(2)}) async-start(bf16[3,3,128,1024]{2,1,0,3:T(4,128)(2,1)} %copy.36), calls=%async_computation.1 | async-start | bytes 6291456 | tf_op jit(solution)/shard_map/all_to_all | solution.py:74
  47.7 117.7 %all-gather.8.cloned.1.call-start = ((), (), s32[]{:S(2)}) async-start(), calls=%async_computation.3 | async-start | bytes 2985984 | tf_op jit(solution)/shard_map/all_gather | solution.py:91
  105.5 1.7 copy-start.9
  105.5 1.7 copy-start.17
  113.8 11.1 %collective-permute-start.3 = (bf16[1,1,64,128]{3,2,1,0:T(8,128)(2,1)S(1)}, bf16[1,1,64,128]{3,2,1,0:T(8,128)(2,1)S(1)}, u32[]{:S(2)}, u32[]{:S(2)}) collective-permute-start(bf16[1,1,64,128]{3,2,1,0:T(8,128)(2,1)S(1)} %slice.126), channel_id=1, source_target_pairs={{8,0},{16,8},{24,16},{32,24},{40,32},{48,40},{56,48},{9,1},{17,9},... | collective-permute-start | bytes 49160 | tf_op jit(solution)/shard_map/ppermute | solution.py:18
  115.1 9.9 %collective-permute-start.2 = (bf16[1,1,64,128]{3,2,1,0:T(8,128)(2,1)S(1)}, bf16[1,1,64,128]{3,2,1,0:T(8,128)(2,1)S(1)}, u32[]{:S(2)}, u32[]{:S(2)}) collective-permute-start(bf16[1,1,64,128]{3,2,1,0:T(8,128)(2,1)S(1)} %slice.123), channel_id=1, source_target_pairs={{0,8},{8,16},{16,24},{24,32},{32,40},{40,48},{48,56},{1,9},{9,17},... | collective-permute-start | bytes 49160 | tf_op jit(solution)/shard_map/ppermute | solution.py:15
  125.9 98.1 %all-gather.10.cloned.1.call-start = ((), (), s32[]{:S(2)}) async-start(), calls=%async_computation.4 | async-start | bytes 2985984 | tf_op jit(solution)/shard_map/all_gather | solution.py:59
  176.6 10.2 %collective-permute-start.5 = (bf16[1,1,64,128]{3,2,1,0:T(8,128)(2,1)S(1)}, bf16[1,1,64,128]{3,2,1,0:T(8,128)(2,1)S(1)}, u32[]{:S(2)}, u32[]{:S(2)}) collective-permute-start(bf16[1,1,64,128]{3,2,1,0:T(8,128)(2,1)S(1)} %slice.132), channel_id=1, source_target_pairs={{8,0},{16,8},{24,16},{32,24},{40,32},{48,40},{56,48},{9,1},{17,9},... | collective-permute-start | bytes 49160 | tf_op jit(solution)/shard_map/ppermute | solution.py:18
  178.0 8.9 %collective-permute-start.4 = (bf16[1,1,64,128]{3,2,1,0:T(8,128)(2,1)S(1)}, bf16[1,1,64,128]{3,2,1,0:T(8,128)(2,1)S(1)}, u32[]{:S(2)}, u32[]{:S(2)}) collective-permute-start(bf16[1,1,64,128]{3,2,1,0:T(8,128)(2,1)S(1)} %slice.129), channel_id=1, source_target_pairs={{0,8},{8,16},{16,24},{24,32},{32,40},{40,48},{48,56},{1,9},{9,17},... | collective-permute-start | bytes 49160 | tf_op jit(solution)/shard_map/ppermute | solution.py:15
  186.0 0.7 copy-start.14
  186.8 40.4 %copy-start.12 = (bf16[16,1,64,128]{3,2,0,1:T(8,128)(2,1)}, bf16[16,1,64,128]{3,2,0,1:T(8,128)(2,1)S(1)}, u32[]{:S(2)}) copy-start(bf16[16,1,64,128]{3,2,0,1:T(8,128)(2,1)S(1)} %copy.70) | copy-start | bytes 786436
  187.7 120.9 %all-gather.12.cloned.1.call-start = ((), (), s32[]{:S(2)}) async-start(), calls=%async_computation.5 | async-start | bytes 2359296 | tf_op jit(solution)/shard_map/all_gather | solution.py:100
  227.8 1.7 copy-start.10
  227.8 1.8 copy-start.15
  236.9 50.0 %copy-start.6 = (bf16[1,18,66,1024]{3,2,1,0:T(8,128)(2,1)S(1)}, bf16[1,18,66,1024]{3,2,1,0:T(8,128)(2,1)}, u32[]{:S(2)}) copy-start(bf16[1,18,66,1024]{3,2,1,0:T(8,128)(2,1)} %all-gather.8.cloned.1.call-done) | copy-start | bytes 7299076
  286.6 206.1 %all-reduce.6.cloned.1.call-start = ((), (), s32[]{:S(2)}) async-start(), calls=%async_computation.6 | async-start | bytes 10461184 | tf_op jit(solution)/shard_map/psum | solution.py:106
  288.7 1.8 copy-start.11
  292.2 1.8 copy-start.7
  292.2 1.7 copy-start.13
  298.0 10.6 %copy-start.3 = (bf16[1,18,66,128]{3,2,1,0:T(8,128)(2,1)S(1)}, bf16[1,18,66,128]{3,2,1,0:T(8,128)(2,1)}, u32[]{:S(2)}) copy-start(bf16[1,18,66,128]{3,2,1,0:T(8,128)(2,1)} %select_maximum_fusion.4) | copy-start | bytes 912388
  308.6 2.2 copy-start.2
  314.8 1.4 copy-start.4
  314.8 1.9 copy-start.5
  492.7 5.3 %copy-start.16 = (f32[1000,128]{1,0:T(8,128)S(1)}, f32[1000,128]{1,0:T(8,128)}, u32[]{:S(2)}) copy-start(f32[1000,128]{1,0:T(8,128)} %get-tuple-element.23) | copy-start | bytes 1536004
  492.7 6.1 %copy-start.1 = (f32[1000,128]{1,0:T(8,128)S(1)}, f32[1000,128]{1,0:T(8,128)}, u32[]{:S(2)}) copy-start(f32[1000,128]{1,0:T(8,128)} %param.6) | copy-start | bytes 1536004
Sparse Core Ops, SparseCore 0:
  38.0 50.9 all-gather.5
  126.0 39.3 all-gather.7
  187.8 36.1 all-gather.9
  286.8 21.7 all-gather.11
  319.5 173.1 all-reduce.5
